TPU v7x, 32 devices: a whole 2x2x4 slice. The times are simulated.
32 devices in a mesh: groups: 2 (over x), wide: 16 (over z, y, core).
Axes of the slice: x: 2, y: 2, z: 4, core: 2. Of those that a mesh axis runs over, the one named last changes fastest.
Arguments:
- kernel_coarse: bfloat16 [128, 32, 2048], P(('groups', 'wide')), parts along dimension 0, may hold values from -6 to 6
- row_coeffs: bfloat16 [2048, 2, 1024], P(('groups', 'wide')), parts along dimension 0, may hold values from -1 to 1
- col_coeffs: bfloat16 [32, 1024], P('groups', 'wide'), parts along dimension 0, may hold values from -1 to 1
- column_coarse: int32 [32], P('groups'), parts along dimension 0, may hold values from 0 to 63
- row_coarse: int32 [2048, 2], P(('groups', 'wide')), parts along dimension 0, may hold values from 0 to 63, as said below
Outputs:
- hamiltonian: float32 [2048, 32, 512], P(('groups', 'wide')), parts along dimension 0
There are 2 independent parts, one for each index of `groups`. A program takes and returns all parts, laid end to end along the dimension named above; each array names one. Nothing has to cross between parts.
Inputs may be any that keep to these rules, and one draw needn't show every extreme that they name: `row_coarse`: coarse row c belongs to owner device c // 4. In each aligned block of 64 fine rows, each owner device is named by either none or exactly 16 of the block's 2 * 64 entries. The 2 entries of one fine row differ.
All inputs are finite; a program needn't handle non-finite values.
Results may differ from a plain program's by a relative error of at most 0.005.
Values may be sent and summed in bfloat16 or wider, within the bound.
A program may use at most 64 MiB of HBM per device.

v0:
```python
import jax
import jax.numpy as jnp
from jax import lax
from jax.sharding import PartitionSpec as P

NVAL = 4
NCOND = 8
NCC = 64


def expand_panel(col_coeffs, column_coarse, pair_width):
    coarse_cols = NCC
    fine_cols = column_coarse.shape[0]
    onehot = (column_coarse[None, :] == jnp.arange(coarse_cols, dtype=jnp.int32)[:, None]).astype(
        jnp.float32
    )
    col_mats = jnp.transpose(
        col_coeffs.astype(jnp.float32).reshape(fine_cols, pair_width, pair_width), (1, 0, 2)
    )
    col_panel = onehot[:, None, :, None] * col_mats[None, :, :, :]
    return col_panel.reshape(coarse_cols * pair_width, fine_cols * pair_width).astype(jnp.bfloat16)


def per_device(kernel_coarse, row_coeffs, col_coeffs, column_coarse, row_coarse):
    pair_width = NVAL * NCOND
    wide_count = lax.axis_size("wide")
    whole_cols = lax.all_gather(col_coeffs, "wide", axis=1, tiled=True)
    col_panel = expand_panel(whole_cols, column_coarse, pair_width)
    owned_rows = kernel_coarse.shape[0]
    tile_width = col_panel.shape[1]
    expanded = jnp.dot(
        kernel_coarse.reshape(owned_rows * pair_width, -1),
        col_panel,
        preferred_element_type=jnp.float32,
    )
    expanded = expanded.astype(jnp.bfloat16).reshape(owned_rows, pair_width, tile_width)
    fine_rows = row_coeffs.shape[0]
    neighbours = row_coeffs.shape[1]
    ref_count = fine_rows * neighbours
    left_coeffs = row_coeffs.reshape(ref_count, pair_width * pair_width)
    coarse_ids = row_coarse.reshape(ref_count)
    slot_cap = max(2, (2 * ref_count + wide_count - 1) // wide_count)
    owner_dev = coarse_ids // owned_rows
    local_row = coarse_ids - owner_dev * owned_rows
    owner_hits = (owner_dev[:, None] == jnp.arange(wide_count, dtype=jnp.int32)[None, :]).astype(
        jnp.int32
    )
    slot_rank = jnp.sum(jnp.cumsum(owner_hits, axis=0) * owner_hits, axis=1) - 1
    slot_place = owner_dev * slot_cap + slot_rank
    outbox = (
        jnp.zeros((wide_count * slot_cap, pair_width * pair_width), jnp.bfloat16)
        .at[slot_place]
        .set(left_coeffs)
    )
    outbox = outbox.reshape(wide_count, slot_cap, pair_width * pair_width)
    slot_rows = jnp.full((wide_count * slot_cap,), -1, jnp.int32).at[slot_place].set(local_row)
    slot_rows = slot_rows.reshape(wide_count, slot_cap)
    got_coeffs = lax.all_to_all(outbox, "wide", split_axis=0, concat_axis=0, tiled=True)
    got_rows = lax.all_to_all(slot_rows, "wide", split_axis=0, concat_axis=0, tiled=True)
    filled = got_rows >= 0
    chosen = expanded[jnp.maximum(got_rows, 0)]
    left_mats = got_coeffs.reshape(got_coeffs.shape[0], got_coeffs.shape[1], pair_width, pair_width)
    fine_tiles = jnp.einsum(
        "nsba,nsbx->nsax", left_mats, chosen, preferred_element_type=jnp.float32
    )
    fine_tiles = jnp.where(filled[:, :, None, None], fine_tiles, jnp.float32(0.0)).astype(
        jnp.bfloat16
    )
    returned = lax.all_to_all(fine_tiles, "wide", split_axis=0, concat_axis=0, tiled=True)
    fine_tiles = returned.reshape(wide_count * slot_cap, pair_width, tile_width)[slot_place]
    summed = jnp.sum(
        fine_tiles.astype(jnp.float32).reshape(fine_rows, neighbours, pair_width, tile_width),
        axis=1,
    )
    return summed


def solution(mesh):
    in_specs = (
        P(("groups", "wide"), None, None),
        P(("groups", "wide"), None, None),
        P("groups", "wide"),
        P("groups"),
        P(("groups", "wide"), None),
    )
    out_specs = P(("groups", "wide"), None, None)
    return jax.shard_map(
        per_device, mesh=mesh, in_specs=in_specs, out_specs=out_specs, check_vma=False
    )
```

profile of v0, /device:TPU:15, one launch (start us, length us, event | category | flops | bytes accessed | tf_op | source)
XLA Modules:
  0.0 275.9 jit_solution(6758745304257496293)
XLA Ops:
  0.0 0.0 copy-start
  0.0 0.8 copy.18
  0.8 0.1 reshape.191
  1.0 0.1 reshape.190
  1.1 0.1 fusion.2
  1.2 0.2 reduce_window_sum.11
  1.4 0.2 select_reduce_fusion
  1.6 1.0 scatter_custom_fusion
  2.6 0.7 all_to_all.12
  3.3 6.6 %all-to-all-start = ((s32[16,1,16]{2,1,0:T(1,128)}), s32[16,1,16]{2,1,0:T(1,128)S(1)}, u32[]{:S(2)}, u32[]{:S(2)}) async-start(s32[16,1,16]{2,1,0:T(1,128)} %all_to_all.12), calls=%async_computation | async-start | bytes 16384 | tf_op jit(solution)/shard_map/all_to_all | solution.py:59
  9.8 0.7 fusion.3
  10.5 15.5 %all-gather = bf16[16,64,16]{1,2,0:T(8,128)(2,1)S(1)} all-gather(bf16[1,64,16]{1,2,0:T(8,128)(2,1)} %bitcast.42), channel_id=1, replica_groups=mesh['groups'=2,'wide'=16] {'wide'}, dimensions={0}, use_global_device_ids=true | all-gather | bytes 34816 | tf_op jit(solution)/shard_map/all_gather | solution.py:27
  26.0 0.1 reshape.237
  26.1 0.1 reshape.200
  26.2 0.2 copy.22
  26.4 1.1 reshape.229
  27.4 2.0 scatter_custom_fusion.1
  29.4 0.0 all-to-all-done
  29.4 10.1 %all-to-all-start.1 = ((bf16[16,16,1024]{2,1,0:T(8,128)(2,1)}), bf16[16,16,1024]{2,1,0:T(8,128)(2,1)S(1)}, u32[]{:S(2)}, u32[]{:S(2)}) async-start(bf16[16,16,1024]{2,1,0:T(8,128)(2,1)} %bitcast.4), calls=%async_computation.1 | async-start | bytes 1048576 | tf_op jit(solution)/shard_map/all_to_all | solution.py:58
  39.5 5.6 %multiply_convert_fusion = bf16[64,32,16,32]{3,2,1,0:T(8,128)(2,1)} fusion(f32[32,16,32]{2,1,0:T(8,128)S(1)} %copy.22, f32[64,16]{1,0:T(8,128)S(1)} %fusion.3), kind=kLoop, calls=%fused_computation.5 | loop fusion | flops 2097152 | bytes 2166784 | tf_op jit(solution)/shard_map/convert_element_type | solution.py:21
  45.0 10.9 %convert_element_type.42 = bf16[2048,512]{1,0:T(8,128)(2,1)S(1)} reshape(bf16[64,32,16,32]{3,2,1,0:T(8,128)(2,1)} %multiply_convert_fusion) | data formatting | bytes 4194304 | tf_op jit(solution)/shard_map/convert_element_type | solution.py:21
  56.0 0.0 copy-done
  56.0 0.5 convolution_convert_fusion
  56.4 0.1 reshape.203
  56.5 8.5 %gather_fusion = bf16[256,32,512]{2,1,0:T(8,128)(2,1)} fusion(bf16[4,32,512]{2,1,0:T(8,128)(2,1)S(1)} %bitcast.36, s32[1024]{0:T(1024)S(1)} %pad_clamp_fusion.1), kind=kCustom, calls=%fused_computation | custom fusion | bytes 16778240 | tf_op jit(solution)/shard_map/gather | solution.py:61
  65.0 0.0 all-to-all-done.1
  65.0 1.6 reshape.194
  66.6 9.2 %select_convert_fusion = bf16[16,16,32,512]{3,2,1,0:T(8,128)(2,1)} fusion(bf16[16,16,32,32]{3,2,1,0:T(8,128)(2,1)S(1)} %reshape.194, bf16[16,16,32,512]{3,2,1,0:T(8,128)(2,1)} %bitcast.37, pred[16,16]{1,0:T(8,128)(4,1)S(1)} %compare_bitcast_fusion), kind=kOutput, calls=%fused_computation.4 | convolution fusion | flops 276824064 | bytes 17301760 | tf_op jit(solution)/shard_map/nsba,nsbx->nsax/dot_general | solution.py:63
  75.8 6.0 %all-to-all-start.2 = ((bf16[16,16,32,512]{3,2,1,0:T(8,128)(2,1)}), bf16[16,16,32,512]{3,2,1,0:T(8,128)(2,1)}, u32[]{:S(2)}, u32[]{:S(2)}) async-start(bf16[16,16,32,512]{3,2,1,0:T(8,128)(2,1)} %select_convert_fusion), calls=%async_computation.2 | async-start | bytes 16777216 | tf_op jit(solution)/shard_map/all_to_all | solution.py:69
  81.8 182.3 %all-to-all-done.2 = bf16[16,16,32,512]{3,2,1,0:T(8,128)(2,1)} async-done(((bf16[16,16,32,512]{3,2,1,0:T(8,128)(2,1)}), bf16[16,16,32,512]{3,2,1,0:T(8,128)(2,1)}, u32[]{:S(2)}, u32[]{:S(2)}) %all-to-all-start.2) | async-done | bytes 8388640 | tf_op jit(solution)/shard_map/all_to_all | solution.py:69
  264.1 6.2 %gather_fusion.1 = bf16[128,32,512]{2,1,0:T(8,128)(2,1)} fusion(bf16[256,32,512]{2,1,0:T(8,128)(2,1)} %bitcast.14, s32[1024]{0:T(1024)S(1)} %pad_clamp_fusion), kind=kCustom, calls=%fused_computation.1 | custom fusion | bytes 8389120 | tf_op jit(solution)/shard_map/gather | solution.py:70
  270.3 5.6 %convert_reduce_fusion = f32[64,32,512]{2,1,0:T(8,128)} fusion(bf16[128,32,512]{2,1,0:T(8,128)(2,1)} %gather_fusion.1), kind=kLoop, calls=%fused_computation.6 | loop fusion | flops 3145728 | bytes 8388608 | tf_op jit(solution)/shard_map/reduce_sum | solution.py:71
  (7 shorter events, 0.1 us)
Async XLA Ops:
  0.0 56.0 %copy-start = (bf16[4,32,2048]{2,1,0:T(8,128)(2,1)S(1)}, bf16[4,32,2048]{2,1,0:T(8,128)(2,1)}, u32[]{:S(2)}) copy-start(bf16[4,32,2048]{2,1,0:T(8,128)(2,1)} %param.5) | copy-start | bytes 1572868
  3.3 26.1 %all-to-all-start = ((s32[16,1,16]{2,1,0:T(1,128)}), s32[16,1,16]{2,1,0:T(1,128)S(1)}, u32[]{:S(2)}, u32[]{:S(2)}) async-start(s32[16,1,16]{2,1,0:T(1,128)} %all_to_all.12), calls=%async_computation | async-start | bytes 16384 | tf_op jit(solution)/shard_map/all_to_all | solution.py:59
  29.4 35.7 %all-to-all-start.1 = ((bf16[16,16,1024]{2,1,0:T(8,128)(2,1)}), bf16[16,16,1024]{2,1,0:T(8,128)(2,1)S(1)}, u32[]{:S(2)}, u32[]{:S(2)}) async-start(bf16[16,16,1024]{2,1,0:T(8,128)(2,1)} %bitcast.4), calls=%async_computation.1 | async-start | bytes 1048576 | tf_op jit(solution)/shard_map/all_to_all | solution.py:58
  75.8 188.3 %all-to-all-start.2 = ((bf16[16,16,32,512]{3,2,1,0:T(8,128)(2,1)}), bf16[16,16,32,512]{3,2,1,0:T(8,128)(2,1)}, u32[]{:S(2)}, u32[]{:S(2)}) async-start(bf16[16,16,32,512]{3,2,1,0:T(8,128)(2,1)} %select_convert_fusion), calls=%async_computation.2 | async-start | bytes 16777216 | tf_op jit(solution)/shard_map/all_to_all | solution.py:69
where the time goes:
time: 277 us; the launch traced here: 276 us
  waiting for transfers between devices  182 us (66%)
  local copies, waits for them, and re-layouts  33.4 us (12%)
  starting transfers between devices  22.6 us (8%)
  blocking collectives  15.5 us (6%)
  other arithmetic  12.3 us (4%)
  matrix products  9.62 us (3%)
    all_to_all x1, waiting for transfers between devices, per_device(): lax.all_to_all(fine_tiles, 'wide', split_axis=0, concat_axis=0, tiled=True)  182 us
    all_gather x1, blocking collectives, per_device(): whole_cols = lax.all_gather(col_coeffs, 'wide', axis=1, tiled=True)  15.5 us
    convert_element_type x1, local copies, waits for them, and re-layouts, expand_panel(): col_panel.reshape(coarse_cols * pair_width, fine_cols * pair_width)  10.9 us
    all_to_all x1, starting transfers between devices, per_device(): lax.all_to_all(outbox, 'wide', split_axis=0, concat_axis=0, tiled=True)  10.1 us
    dot_general x1, matrix products, per_device(): jnp.einsum('nsba,nsbx->nsax', left_mats, chosen, preferred_element_type=j...  9.16 us
    gather x1, local copies, waits for them, and re-layouts, per_device(): chosen = expanded[jnp.maximum(got_rows, 0)]  8.5 us
    all_to_all x1, starting transfers between devices, per_device(): lax.all_to_all(slot_rows, 'wide', split_axis=0, concat_axis=0, tiled=True)  6.55 us
    gather x1, local copies, waits for them, and re-layouts, per_device(): returned.reshape(wide_count * slot_cap, pair_width, tile_width)[slot_place]  6.17 us
  transfers between devices with their start and end apart: 3, of which 1 were waited for; matrix products, arithmetic and copies ran while one was open for 11% of the time, Pallas kernels for 0%

commit v1 on v0

v1 whole, which is shorter than its diff:
```python
import functools

import jax
import jax.numpy as jnp
from jax import lax
from jax.experimental import pallas as pl
from jax.experimental.pallas import tpu as pltpu
from jax.sharding import PartitionSpec as P

PAIR = 32
NCC = 64


def expand_panel(col_coeffs, column_coarse):
    fine_cols = column_coarse.shape[0]
    onehot = (column_coarse[None, :] == jnp.arange(NCC, dtype=jnp.int32)[:, None]).astype(jnp.bfloat16)
    col_mats = jnp.transpose(col_coeffs.reshape(fine_cols, PAIR, PAIR), (1, 0, 2))
    col_panel = onehot[:, None, :, None] * col_mats[None, :, :, :]
    return col_panel.reshape(NCC * PAIR, fine_cols * PAIR)


def fine_kernel(per_step, picks_ref, expanded_ref, left_ref, out_ref):
    step = pl.program_id(0)
    for u in range(per_step):
        row = step * per_step + u
        first = pl.multiple_of(picks_ref[2 * row] * PAIR, PAIR)
        second = pl.multiple_of(picks_ref[2 * row + 1] * PAIR, PAIR)
        chosen = jnp.concatenate(
            [expanded_ref[pl.ds(first, PAIR), :], expanded_ref[pl.ds(second, PAIR), :]], axis=0
        )
        out_ref[u] = jnp.dot(
            left_ref[u * PAIR : (u + 1) * PAIR, :], chosen, preferred_element_type=jnp.float32
        )


def fine_rows_of(picks, expanded, left):
    fine_rows = picks.shape[0] // 2
    width = expanded.shape[1]
    per_step = 8
    return pl.pallas_call(
        functools.partial(fine_kernel, per_step),
        grid_spec=pltpu.PrefetchScalarGridSpec(
            num_scalar_prefetch=1,
            grid=(fine_rows // per_step,),
            in_specs=[
                pl.BlockSpec(memory_space=pltpu.VMEM),
                pl.BlockSpec((per_step * PAIR, 2 * PAIR), lambda s, picks: (s, 0)),
            ],
            out_specs=pl.BlockSpec((per_step, PAIR, width), lambda s, picks: (s, 0, 0)),
        ),
        out_shape=jax.ShapeDtypeStruct((fine_rows, PAIR, width), jnp.float32),
        compiler_params=pltpu.CompilerParams(vmem_limit_bytes=48 * 1024 * 1024),
        name="fine_rows",
    )(picks, expanded, left)


def per_device(kernel_coarse, row_coeffs, col_coeffs, column_coarse, row_coarse):
    whole_cols = lax.all_gather(col_coeffs, "wide", axis=1, tiled=True)
    col_panel = expand_panel(whole_cols, column_coarse)
    owned = kernel_coarse.shape[0] * PAIR
    expanded = jnp.dot(
        kernel_coarse.reshape(owned, -1), col_panel, preferred_element_type=jnp.float32
    ).astype(jnp.bfloat16)
    expanded = lax.all_gather(expanded, "wide", axis=0, tiled=True)
    fine_rows = row_coeffs.shape[0]
    left = row_coeffs.reshape(fine_rows, 2, PAIR, PAIR).transpose(0, 3, 1, 2)
    left = left.reshape(fine_rows * PAIR, 2 * PAIR)
    return fine_rows_of(row_coarse.reshape(-1), expanded, left)


def solution(mesh):
    in_specs = (
        P(("groups", "wide"), None, None),
        P(("groups", "wide"), None, None),
        P("groups", "wide"),
        P("groups"),
        P(("groups", "wide"), None),
    )
    out_specs = P(("groups", "wide"), None, None)
    return jax.shard_map(
        per_device, mesh=mesh, in_specs=in_specs, out_specs=out_specs, check_vma=False
    )
```

time: 277 us -> 99.6 us (0.36)
  the two profiles are of different devices: /device:TPU:15 before, /device:TPU:0 now
where the time goes in v1:
time: 99.6 us; the launch traced here: 99.2 us
  waiting for transfers between devices  36.6 us (37%)
  blocking collectives  23.6 us (24%)
  local copies, waits for them, and re-layouts  15.1 us (15%)
  between operations  13.5 us (14%)
  Pallas kernels  4.81 us (5%)
  other arithmetic  4.51 us (5%)
  matrix products  1.11 us (1%)
    all_gather x1, waiting for transfers between devices, per_device(): expanded = lax.all_gather(expanded, 'wide', axis=0, tiled=True)  36.6 us
    all_gather x1, blocking collectives, per_device(): whole_cols = lax.all_gather(col_coeffs, 'wide', axis=1, tiled=True)  23.6 us
    mul x1, local copies, waits for them, and re-layouts, expand_panel(): col_panel = onehot[:, None, :, None] * col_mats[None, :, :, :]  10.9 us
    pallas_call x1, Pallas kernels, fine_rows_of(): pl.pallas_call(functools.partial(fine_kernel, per_step), grid_spec=pltpu....  4.81 us
    mul x1, other arithmetic, expand_panel(): col_panel = onehot[:, None, :, None] * col_mats[None, :, :, :]  3.84 us
    unnamed x11, local copies, waits for them, and re-layouts  2.12 us
  transfers between devices with their start and end apart: 1, of which 1 were waited for; matrix products, arithmetic and copies ran while one was open for 2% of the time, Pallas kernels for 0%

profile of v1, /device:TPU:0, one launch (start us, length us, event | category | flops | bytes accessed | tf_op | source)
XLA Modules:
  0.0 99.2 jit_solution(5369179407978013756)
XLA Ops:
  6.5 0.0 copy-start
  6.5 0.0 all-gather.3.cloned.1.call-start
  6.5 23.6 %all-gather = bf16[16,64,16]{1,2,0:T(8,128)(2,1)S(1)} all-gather(bf16[1,64,16]{1,2,0:T(8,128)(2,1)} %bitcast.21), channel_id=1, replica_groups=mesh['groups'=2,'wide'=16] {'wide'}, dimensions={0}, use_global_device_ids=true | all-gather | bytes 34816 | tf_op jit(solution)/shard_map/all_gather | solution.py:58
  30.2 0.1 reshape.54
  30.3 0.1 reshape.49
  30.5 0.1 copy.18
  30.5 0.7 fusion.1
  31.2 3.8 %broadcast_multiply_fusion = bf16[64,32,16,32]{3,2,1,0:T(8,128)(2,1)} fusion(bf16[32,16,32]{2,1,0:T(8,128)(2,1)S(1)} %copy.18, bf16[64,16]{1,0:T(8,128)(2,1)S(1)} %fusion.1), kind=kLoop, calls=%fused_computation | loop fusion | flops 1048576 | bytes 2131968 | tf_op jit(solution)/shard_map/mul | solution.py:18
  35.0 0.0 copy-start.2
  35.0 10.9 %mul.26 = bf16[2048,512]{1,0:T(8,128)(2,1)S(1)} reshape(bf16[64,32,16,32]{3,2,1,0:T(8,128)(2,1)} %broadcast_multiply_fusion) | data formatting | bytes 4194304 | tf_op jit(solution)/shard_map/mul | solution.py:18
  46.0 0.0 copy-done
  46.0 0.0 copy-start.3
  46.0 1.1 %fusion = bf16[128,512]{1,0:T(8,128)(2,1)} fusion(bf16[128,2048]{1,0:T(8,128)(2,1)S(1)} %bitcast.17, bf16[2048,512]{1,0:T(8,128)(2,1)S(1)} %mul.26), kind=kOutput, calls=%fused_computation.2 | convolution fusion | flops 268500992 | bytes 2752512 | tf_op jit(solution)/shard_map/dot_general | solution.py:61
  47.1 0.0 all-gather.3.cloned.1.call-update
  47.1 0.0 copy-done.2
  47.1 0.3 copy.20
  47.5 1.2 %copy.24 = bf16[64,32,2,32]{3,2,1,0:T(2,128)(2,1)S(1)} copy(bf16[64,32,2,32]{0,1,3,2:T(8,128)(2,1)S(1)} %bitcast.18) | data formatting | bytes 524288 | tf_op jit(solution)/shard_map/reshape | solution.py:67
  48.7 0.5 reshape.55.left_ref
  49.1 0.0 copy-done.3
  49.1 0.1 copy.16
  49.2 0.1 reshape.48.picks_ref
  49.4 36.6 %all-gather.3.cloned.1.call-done.expanded_ref = bf16[2048,512]{1,0:T(8,128)(2,1)} async-done(((bf16[128,512]{1,0:T(8,128)(2,1)}), bf16[2048,512]{1,0:T(8,128)(2,1)}) %all-gather.3.cloned.1.call-update) | async-done | bytes 2097168 | tf_op jit(solution)/shard_map/all_gather | solution.py:64
  86.0 0.0 copy-start.1
  86.0 1.6 %copy-done.1 = bf16[2048,512]{1,0:T(8,128)(2,1)S(1)} copy-done((bf16[2048,512]{1,0:T(8,128)(2,1)S(1)}, bf16[2048,512]{1,0:T(8,128)(2,1)}, u32[]{:S(2)}) %copy-start.1) | copy-done | bytes 2097176
  87.6 4.8 %fine_rows.1 = f32[64,32,512]{2,1,0:T(8,128)} custom-call(s32[128]{0:T(128)S(1)} %reshape.48.picks_ref, bf16[2048,512]{1,0:T(8,128)(2,1)S(1)} %copy-done.1, bf16[2048,64]{1,0:T(8,128)(2,1)S(1)} %reshape.55.left_ref), custom_call_target="tpu_custom_call" | custom-call | tf_op jit(solution)/shard_map/fine_rows/pallas_call | solution.py:40
  (1 shorter events, 0.0 us)
Async XLA Ops:
  6.5 39.4 %copy-start = (bf16[4,32,2048]{2,1,0:T(8,128)(2,1)S(1)}, bf16[4,32,2048]{2,1,0:T(8,128)(2,1)}, u32[]{:S(2)}) copy-start(bf16[4,32,2048]{2,1,0:T(8,128)(2,1)} %param.5) | copy-start | bytes 1572868
  6.5 79.4 %all-gather.3.cloned.1.call-start = ((), (), s32[]{:S(2)}) async-start(), calls=%async_computation | async-start | bytes 2228224 | tf_op jit(solution)/shard_map/all_gather | solution.py:64
  35.0 12.1 %copy-start.2 = (bf16[64,2,1024]{2,1,0:T(2,128)(2,1)S(1)}, bf16[64,2,1024]{2,1,0:T(2,128)(2,1)}, u32[]{:S(2)}) copy-start(bf16[64,2,1024]{2,1,0:T(2,128)(2,1)} %param.6) | copy-start | bytes 786436
  46.0 3.1 %copy-start.3 = (s32[64,2]{0,1:T(2,128)S(1)}, s32[64,2]{0,1:T(2,128)}, u32[]{:S(2)}) copy-start(s32[64,2]{0,1:T(2,128)} %param.9) | copy-start | bytes 1540
  86.0 1.6 %copy-start.1 = (bf16[2048,512]{1,0:T(8,128)(2,1)S(1)}, bf16[2048,512]{1,0:T(8,128)(2,1)}, u32[]{:S(2)}) copy-start(bf16[2048,512]{1,0:T(8,128)(2,1)} %all-gather.3.cloned.1.call-done.expanded_ref) | copy-start | bytes 6291460
Sparse Core Ops, SparseCore 0:
  47.3 38.6 all-gather.2

commit v2 on v1

--- a/solution.py
+++ b/solution.py
@@ -8,15 +8,7 @@
 from jax.sharding import PartitionSpec as P
 
 PAIR = 32
-NCC = 64
-
-
-def expand_panel(col_coeffs, column_coarse):
-    fine_cols = column_coarse.shape[0]
-    onehot = (column_coarse[None, :] == jnp.arange(NCC, dtype=jnp.int32)[:, None]).astype(jnp.bfloat16)
-    col_mats = jnp.transpose(col_coeffs.reshape(fine_cols, PAIR, PAIR), (1, 0, 2))
-    col_panel = onehot[:, None, :, None] * col_mats[None, :, :, :]
-    return col_panel.reshape(NCC * PAIR, fine_cols * PAIR)
+MESH = pl.DeviceIdType.MESH
 
 
 def fine_kernel(per_step, picks_ref, expanded_ref, left_ref, out_ref):
@@ -54,14 +46,275 @@
     )(picks, expanded, left)
 
 
+def ring_place(chip, chips):
+    rung, side = lax.div(chip, 2), lax.rem(chip, 2)
+    return (1 - side) * rung + side * (chips - 1 - rung)
+
+
+def chip_at(place, chips):
+    place = lax.rem(place + 2 * chips, chips)
+    side = lax.div(place, chips // 2)
+    return (1 - side) * (2 * place) + side * (2 * (chips - 1 - place) + 1)
+
+
+def iota(shape, dim):
+    return lax.broadcasted_iota(jnp.int32, shape, dim)
+
+
+def ones_where(mask):
+    return jnp.where(mask, 1.0, 0.0).astype(jnp.bfloat16)
+
+
+def pick_kernel(column_ref, coarse_ref, picked_ref):
+    lane_gap = iota((128, 128), 0) - iota((128, 128), 1)
+    lane_group = lax.div(iota((128, 128), 1), PAIR)
+    for block in range(picked_ref.shape[1] // 128):
+        sources, moves = [], []
+        for j in range(4):
+            coarse = column_ref[4 * block + j]
+            wide_block = lax.div(coarse, 4)
+            offset = (coarse - 4 * wide_block - j) * PAIR
+            sources.append(coarse_ref[:, pl.ds(pl.multiple_of(wide_block * 128, 128), 128)])
+            moves.append(ones_where((lane_group == j) & (lane_gap == offset)))
+        picked_ref[:, block * 128 : (block + 1) * 128] = jnp.dot(
+            jnp.concatenate(sources, axis=1),
+            jnp.concatenate(moves, axis=0),
+            preferred_element_type=jnp.float32,
+        ).astype(jnp.bfloat16)
+
+def pick(column_coarse, coarse):
+    return pl.pallas_call(
+        pick_kernel,
+        out_shape=jax.ShapeDtypeStruct(
+            (coarse.shape[0], column_coarse.shape[0] * PAIR), jnp.bfloat16
+        ),
+        in_specs=[pl.BlockSpec(memory_space=pltpu.SMEM), pl.BlockSpec(memory_space=pltpu.VMEM)],
+        out_specs=pl.BlockSpec(memory_space=pltpu.VMEM),
+        name="pick",
+    )(column_coarse, coarse)
+
+
+def exchange_kernel(
+    n, piece, block_ref, cols_ref, expanded_ref,
+    picked, cols, right0, right1, spread,
+    cols_send, cols_recv, ring_send, ring_recv, twin_send, twin_recv,
+):
+    me = lax.axis_index("wide")
+    chips = n // 2
+    core = lax.rem(me, 2)
+    place = ring_place(lax.div(me, 2), chips)
+    twin = me + 1 - 2 * core
+    ahead = 2 * chip_at(place + 1, chips) + core
+    behind = 2 * chip_at(place - 1, chips) + core
+    targets = (ahead, behind)
+    rows, width = picked.shape[1], picked.shape[2]
+    half = rows // 2
+    fine_cols = width // PAIR
+    far = chips // 2
+
+    def peer(k):
+        return lax.rem(me + k, n)
+
+    barrier = pltpu.get_barrier_semaphore()
+
+    def greet(k, carry):
+        pl.semaphore_signal(barrier, inc=1, device_id={"wide": peer(k)}, device_id_type=MESH)
+        return carry
+
+    lax.fori_loop(1, n, greet, 0)
+
+    picked[me] = block_ref[...]
+    cols[pl.ds(pl.multiple_of(me * fine_cols, fine_cols), fine_cols), :] = cols_ref[...]
+
+    pl.semaphore_wait(barrier, n - 1)
+
+    def ring_copy(way, dist, part, source):
+        spot = picked.at[source, pl.ds(part * half, half)]
+        return pltpu.make_async_remote_copy(
+            src_ref=spot, dst_ref=spot,
+            send_sem=ring_send.at[way, dist - 1, part],
+            recv_sem=ring_recv.at[way, dist - 1, part],
+            device_id={"wide": targets[way]}, device_id_type=MESH,
+        )
+
+    def twin_copy(way, dist, part, source):
+        spot = picked.at[source, pl.ds(part * half, half)]
+        return pltpu.make_async_remote_copy(
+            src_ref=spot, dst_ref=spot,
+            send_sem=twin_send.at[way, dist, part],
+            recv_sem=twin_recv.at[way, dist, part],
+            device_id={"wide": twin}, device_id_type=MESH,
+        )
+
+    def cols_copy(k, source):
+        spot = cols.at[pl.ds(pl.multiple_of(source * fine_cols, fine_cols), fine_cols), :]
+        return pltpu.make_async_remote_copy(
+            src_ref=spot, dst_ref=spot,
+            send_sem=cols_send.at[k - 1], recv_sem=cols_recv.at[k - 1],
+            device_id={"wide": peer(k)}, device_id_type=MESH,
+        )
+
+    sent = []
+
+    def start(copy):
+        copy.start()
+        sent.append(copy)
+
+    for turn in range(2):
+        for way in range(2):
+            if far > 1 or (turn ^ way) == way:
+                start(ring_copy(way, 1, turn ^ way, me))
+
+    def send_cols(k, carry):
+        cols_copy(k, me).start()
+        return carry
+
+    lax.fori_loop(1, n, send_cols, 0)
+    for part in range(2):
+        start(twin_copy(0, 0, part, me))
+
+    def wait_cols():
+        def wait_one(k, carry):
+            cols_copy(k, lax.rem(me - k + n, n)).wait_recv()
+            return carry
+
+        lax.fori_loop(1, n, wait_one, 0)
+
+    groups = max(piece, PAIR) // min(piece, PAIR)
+
+    def spread_cols():
+        lane, target = iota((128, width), 0), lax.rem(iota((128, width), 1), PAIR)
+        for g in range(groups):
+            if piece >= PAIR:
+                take = lane == PAIR * g + target
+            else:
+                take = (target == piece * g + lane) & (lane < piece)
+            spread[g] = jnp.dot(
+                cols[...], ones_where(take), preferred_element_type=jnp.float32
+            ).astype(jnp.bfloat16)
+
+    def form_right(side, right):
+        shape = (width // 2, n * fine_cols)
+        row, col = iota(shape, 0) + side * (width // 2), iota(shape, 1)
+        fine, pair = lax.div(row, PAIR), lax.rem(row, PAIR)
+        device, fine_from = lax.div(col, fine_cols), lax.rem(col, fine_cols)
+        total = None
+        for g in range(groups):
+            if piece >= PAIR:
+                take = (fine == fine_from) & (pair == groups * device + g)
+            else:
+                take = (fine == fine_from) & (device == groups * pair + g)
+            term = jnp.dot(
+                ones_where(take),
+                spread[g, :, side * (width // 2) : (side + 1) * (width // 2)],
+                preferred_element_type=jnp.float32,
+            )
+            total = term if total is None else total + term
+        square = (width // 2, width // 2)
+        same = lax.div(iota(square, 0), PAIR) == lax.div(iota(square, 1), PAIR)
+        right[...] = jnp.where(same, total, 0.0).astype(jnp.bfloat16)
+
+    def multiply(source, part):
+        block = picked[source, pl.ds(part * half, half), :]
+        at = pl.ds(pl.multiple_of(source * rows + part * half, half), half)
+        for side, right in enumerate((right0, right1)):
+            span = slice(side * (width // 2), (side + 1) * (width // 2))
+            expanded_ref[at, span] = jnp.dot(
+                block[:, span], right[...], preferred_element_type=jnp.float32
+            ).astype(jnp.bfloat16)
+
+    def own_work():
+        multiply(me, 0)
+        multiply(me, 1)
+
+    def twin_work(way, dist, part, source):
+        twin_copy(way, dist, part, source).wait_recv()
+        multiply(source, part)
+
+    def first_cols():
+        wait_cols()
+        spread_cols()
+
+    work = [
+        first_cols,
+        functools.partial(form_right, 0, right0),
+        functools.partial(form_right, 1, right1),
+        own_work,
+        functools.partial(twin_work, 0, 0, 0, twin),
+        functools.partial(twin_work, 0, 0, 1, twin),
+    ]
+    for dist in range(1, far + 1):
+        for turn in range(2):
+            due = []
+            for way in range(2):
+                part = turn ^ way
+                if dist == far and part != way:
+                    continue
+                chip = chip_at(place + (dist if way else -dist), chips)
+                mine, other = 2 * chip + core, 2 * chip + 1 - core
+                ring_copy(way, dist, part, mine).wait_recv()
+                if dist + 1 < far or (dist + 1 == far and part == way):
+                    start(ring_copy(way, dist + 1, part, mine))
+                start(twin_copy(way, dist, part, mine))
+                due.append(functools.partial(multiply, mine, part))
+                due.append(functools.partial(twin_work, way, dist, part, other))
+            own, theirs = due[0::2], due[1::2]
+            for _ in range(4 if work else 0):
+                if work:
+                    work.pop(0)()
+            work += own + theirs
+    for step in work:
+        step()
+    for copy in sent:
+        copy.wait_send()
+
+    def wait_sent(k, carry):
+        cols_copy(k, me).wait_send()
+        return carry
+
+    lax.fori_loop(1, n, wait_sent, 0)
+
+
+def exchange(block, cols, n, piece):
+    rows, width = block.shape
+    fine_cols = cols.shape[0]
+    far = n // 4
+    groups = max(piece, PAIR) // min(piece, PAIR)
+    total = n * rows * width * 2
+    return pl.pallas_call(
+        functools.partial(exchange_kernel, n, piece),
+        out_shape=jax.ShapeDtypeStruct((n * rows, width), jnp.bfloat16),
+        in_specs=[
+            pl.BlockSpec(memory_space=pltpu.VMEM),
+            pl.BlockSpec(memory_space=pltpu.VMEM),
+        ],
+        out_specs=pl.BlockSpec(memory_space=pltpu.VMEM),
+        scratch_shapes=[
+            pltpu.VMEM((n, rows, width), jnp.bfloat16),
+            pltpu.VMEM((n * fine_cols, 128), jnp.bfloat16),
+            pltpu.VMEM((width // 2, width // 2), jnp.bfloat16),
+            pltpu.VMEM((width // 2, width // 2), jnp.bfloat16),
+            pltpu.VMEM((groups, n * fine_cols, width), jnp.bfloat16),
+            pltpu.SemaphoreType.DMA((n - 1,)),
+            pltpu.SemaphoreType.DMA((n - 1,)),
+            pltpu.SemaphoreType.DMA((2, far, 2)),
+            pltpu.SemaphoreType.DMA((2, far, 2)),
+            pltpu.SemaphoreType.DMA((2, far + 1, 2)),
+            pltpu.SemaphoreType.DMA((2, far + 1, 2)),
+        ],
+        compiler_params=pltpu.CompilerParams(
+            collective_id=0, has_side_effects=True, vmem_limit_bytes=2 * total + 12 * 1024 * 1024 + n * 64 * 1024
+        ),
+        name="exchange",
+    )(block, cols)
+
+
 def per_device(kernel_coarse, row_coeffs, col_coeffs, column_coarse, row_coarse):
-    whole_cols = lax.all_gather(col_coeffs, "wide", axis=1, tiled=True)
-    col_panel = expand_panel(whole_cols, column_coarse)
-    owned = kernel_coarse.shape[0] * PAIR
-    expanded = jnp.dot(
-        kernel_coarse.reshape(owned, -1), col_panel, preferred_element_type=jnp.float32
-    ).astype(jnp.bfloat16)
-    expanded = lax.all_gather(expanded, "wide", axis=0, tiled=True)
+    n = lax.axis_size("wide")
+    piece = col_coeffs.shape[1]
+    cols = jnp.pad(col_coeffs, ((0, 0), (0, 128 - piece)))
+    coarse = kernel_coarse.reshape(kernel_coarse.shape[0] * PAIR, -1)
+    expanded = exchange(pick(column_coarse, coarse), cols, n, piece)
     fine_rows = row_coeffs.shape[0]
     left = row_coeffs.reshape(fine_rows, 2, PAIR, PAIR).transpose(0, 3, 1, 2)
     left = left.reshape(fine_rows * PAIR, 2 * PAIR)

time: 99.6 us -> 36.1 us (0.36)
  waiting for transfers between devices: 36.6 us -> 0 us
  Pallas kernels: 4.81 us -> 30.4 us
  blocking collectives: 23.6 us -> 0 us
  between operations: 13.5 us -> 0.04 us
  local copies, waits for them, and re-layouts: 15.1 us -> 5.43 us
  other arithmetic: 4.51 us -> 0 us
  matrix products: 1.11 us -> 0 us
    all_gather x1 -> x0, waiting for transfers between devices: 36.6 us -> none  [per_device(): expanded = lax.all_gather(expanded, 'wide', axis=0, tiled=True)]
    pallas_call x0 -> x2, Pallas kernels: none -> 25.6 us  [the longest x1 23.5 us: exchange(): pl.pallas_call(functools.partial(exchange_kernel, n, piece), out_shape=ja...]
    all_gather x1 -> x0, blocking collectives: 23.6 us -> none  [per_device(): whole_cols = lax.all_gather(col_coeffs, 'wide', axis=1, tiled=True)]
    mul x1 -> x0, local copies, waits for them, and re-layouts: 10.9 us -> none  [expand_panel(): col_panel = onehot[:, None, :, None] * col_mats[None, :, :, :]]
    mul x1 -> x0, other arithmetic: 3.84 us -> none  [expand_panel(): col_panel = onehot[:, None, :, None] * col_mats[None, :, :, :]]
    dot_general x1 -> x0, matrix products: 1.11 us -> none  [per_device(): jnp.dot(kernel_coarse.reshape(owned, -1), col_panel, preferred_element_ty...]
    unnamed x11 -> x4, local copies, waits for them, and re-layouts: 2.12 us -> 2.92 us
  transfers between devices with their start and end apart: 1 -> 0, of which waited for: 1 -> 0; matrix products, arithmetic and copies ran while one was open for 2% -> 0% of each run, Pallas kernels for 0% -> 0%
where the time goes in v2:
time: 36.1 us; the launch traced here: 35.9 us
  Pallas kernels  30.4 us (84%)
  local copies, waits for them, and re-layouts  5.43 us (15%)
    pallas_call x1, Pallas kernels, exchange(): pl.pallas_call(functools.partial(exchange_kernel, n, piece), out_shape=ja...  23.5 us
    pallas_call x1, Pallas kernels, fine_rows_of(): pl.pallas_call(functools.partial(fine_kernel, per_step), grid_spec=pltpu....  4.81 us
    unnamed x4, local copies, waits for them, and re-layouts  2.92 us
    pallas_call x1, Pallas kernels, pick(): pl.pallas_call(pick_kernel, out_shape=jax.ShapeDtypeStruct((coarse.shape[...  2.02 us
    reshape x2, local copies, waits for them, and re-layouts, per_device(): left = left.reshape(fine_rows * PAIR, 2 * PAIR)  1.68 us

profile of v2, /device:TPU:0, one launch (start us, length us, event | category | flops | bytes accessed | tf_op | source)
XLA Modules:
  0.0 35.9 jit_solution(8804538850940989104)
XLA Ops:
  0.0 0.7 %pad.4.cols_ref = bf16[16,128]{1,0:T(8,128)(2,1)S(1)} pad(bf16[16,64]{1,0:T(8,128)(2,1)} %param.7, bf16[]{:T(256)} %constant.2.clone.1), padding=0_0x0_64 | pad | bytes 6146 | tf_op jit(solution)/shard_map/jit(_pad)/pad | solution.py:315
  0.7 0.8 %copy.8 = s32[64,2]{1,0:T(8,128)S(1)} copy(s32[64,2]{0,1:T(2,128)} %param.9) | data formatting | bytes 1024 | tf_op args[4]
  1.5 0.1 reshape.12.picks_ref
  1.6 2.0 %pick.1.block_ref = bf16[128,512]{1,0:T(8,128)(2,1)} custom-call(s32[16]{0:T(128)} %column_ref.1, bf16[128,2048]{1,0:T(8,128)(2,1)} %bitcast.5), custom_call_target="tpu_custom_call" | custom-call | tf_op jit(solution)/shard_map/pick/pallas_call | solution.py:86
  3.6 1.3 %copy.9 = bf16[64,2,1024]{0,2,1:T(8,128)(2,1)S(1)} copy(bf16[64,2,1024]{2,1,0:T(2,128)(2,1)} %param.6) | data formatting | bytes 524288 | tf_op args[1]
  4.9 1.2 %copy.12 = bf16[64,32,2,32]{3,2,1,0:T(2,128)(2,1)S(1)} copy(bf16[64,32,2,32]{0,1,3,2:T(8,128)(2,1)S(1)} %bitcast.4) | data formatting | bytes 524288 | tf_op jit(solution)/shard_map/reshape | solution.py:320
  6.1 0.5 %reshape.16.left_ref = bf16[2048,64]{1,0:T(8,128)(2,1)S(1)} reshape(bf16[64,32,2,32]{3,2,1,0:T(2,128)(2,1)S(1)} %copy.12) | data formatting | bytes 524288 | tf_op jit(solution)/shard_map/reshape | solution.py:320
  6.6 0.0 copy-start
  6.6 0.9 %copy-done = bf16[128,512]{1,0:T(8,128)(2,1)S(1)} copy-done((bf16[128,512]{1,0:T(8,128)(2,1)S(1)}, bf16[128,512]{1,0:T(8,128)(2,1)}, u32[]{:S(2)}) %copy-start) | copy-done | bytes 131096
  7.5 23.5 %exchange.1.expanded_ref = bf16[2048,512]{1,0:T(8,128)(2,1)S(1)} custom-call(bf16[128,512]{1,0:T(8,128)(2,1)S(1)} %copy-done, bf16[16,128]{1,0:T(8,128)(2,1)S(1)} %pad.4.cols_ref), custom_call_target="tpu_custom_call" | custom-call | tf_op jit(solution)/shard_map/exchange/pallas_call | solution.py:284
  31.0 4.8 %fine_rows.1 = f32[64,32,512]{2,1,0:T(8,128)} custom-call(s32[128]{0:T(128)S(1)} %reshape.12.picks_ref, bf16[2048,512]{1,0:T(8,128)(2,1)S(1)} %exchange.1.expanded_ref, bf16[2048,64]{1,0:T(8,128)(2,1)S(1)} %reshape.16.left_ref), custom_call_target="tpu_custom_call" | custom-call | tf_op jit(solution)/shard_map/fine_rows/pallas_call | solution.py:32
Async XLA Ops:
  6.6 0.9 %copy-start = (bf16[128,512]{1,0:T(8,128)(2,1)S(1)}, bf16[128,512]{1,0:T(8,128)(2,1)}, u32[]{:S(2)}) copy-start(bf16[128,512]{1,0:T(8,128)(2,1)} %pick.1.block_ref) | copy-start | bytes 393220

commit v3 on v1

v3 whole, which is shorter than its diff:
```python
import functools

import jax
import jax.numpy as jnp
from jax import lax
from jax.experimental import pallas as pl
from jax.experimental.pallas import tpu as pltpu
from jax.sharding import PartitionSpec as P

PAIR = 32
COL_ROWS = 16
MESH = pl.DeviceIdType.MESH


def iota(shape, dim):
    return lax.broadcasted_iota(jnp.int32, shape, dim)


def ones_where(mask):
    return jnp.where(mask, 1.0, 0.0).astype(jnp.bfloat16)


def pick_kernel(column_ref, coarse_ref, picked_ref):
    lane_gap = iota((128, 128), 0) - iota((128, 128), 1)
    lane_group = lax.div(iota((128, 128), 1), PAIR)
    for block in range(picked_ref.shape[1] // 128):
        sources, moves = [], []
        for j in range(4):
            coarse = column_ref[4 * block + j]
            wide_block = lax.div(coarse, 4)
            offset = (coarse - 4 * wide_block - j) * PAIR
            sources.append(coarse_ref[:, pl.ds(pl.multiple_of(wide_block * 128, 128), 128)])
            moves.append(ones_where((lane_group == j) & (lane_gap == offset)))
        picked_ref[:, block * 128 : (block + 1) * 128] = jnp.dot(
            jnp.concatenate(sources, axis=1),
            jnp.concatenate(moves, axis=0),
            preferred_element_type=jnp.float32,
        ).astype(jnp.bfloat16)

def pick(column_coarse, coarse):
    return pl.pallas_call(
        pick_kernel,
        out_shape=jax.ShapeDtypeStruct(
            (coarse.shape[0], column_coarse.shape[0] * PAIR), jnp.bfloat16
        ),
        in_specs=[pl.BlockSpec(memory_space=pltpu.SMEM), pl.BlockSpec(memory_space=pltpu.VMEM)],
        out_specs=pl.BlockSpec(memory_space=pltpu.VMEM),
        name="pick",
    )(column_coarse, coarse)


def spread_cols(piece, gathered_ref, spread, right):
    n, fine_cols = gathered_ref.shape[0], COL_ROWS
    width = gathered_ref.shape[2]
    rows = gathered_ref.shape[1] - fine_cols
    side_width = right.shape[1]
    groups = spread.shape[0]
    cols = gathered_ref[:, rows:, 0:128].reshape(n * fine_cols, 128)
    lane, target = iota((128, width), 0), lax.rem(iota((128, width), 1), PAIR)
    for g in range(groups):
        if piece >= PAIR:
            take = lane == PAIR * g + target
        else:
            take = (target == piece * g + lane) & (lane < piece)
        spread[g] = jnp.dot(
            cols, ones_where(take), preferred_element_type=jnp.float32
        ).astype(jnp.bfloat16)
    for side in range(right.shape[0]):
        shape = (side_width, n * fine_cols)
        row, col = iota(shape, 0) + side * side_width, iota(shape, 1)
        fine, pair = lax.div(row, PAIR), lax.rem(row, PAIR)
        device, fine_from = lax.div(col, fine_cols), lax.rem(col, fine_cols)
        total = None
        for g in range(groups):
            if piece >= PAIR:
                take = (fine == fine_from) & (pair == groups * device + g)
            else:
                take = (fine == fine_from) & (device == groups * pair + g)
            term = jnp.dot(
                ones_where(take),
                spread[g, :, side * side_width : (side + 1) * side_width],
                preferred_element_type=jnp.float32,
            )
            total = term if total is None else total + term
        square = (side_width, side_width)
        same = lax.div(iota(square, 0), PAIR) == lax.div(iota(square, 1), PAIR)
        right[side] = jnp.where(same, total, 0.0).astype(jnp.bfloat16)


def fine_kernel(
    per_step, fine_rows, piece, picks_ref, gathered_ref, left_ref, out_ref, spread, right, half_done
):
    step = pl.program_id(0)
    owned = (gathered_ref.shape[1] - COL_ROWS) // PAIR
    side_width = right.shape[1]

    @pl.when(step == 0)
    def _():
        spread_cols(piece, gathered_ref, spread, right)

    def rows_of(coarse):
        owner = lax.div(coarse, owned)
        first = pl.multiple_of((coarse - owner * owned) * PAIR, PAIR)
        return gathered_ref[owner, pl.ds(first, PAIR), :]

    for u in range(per_step):
        row = step * per_step + u
        chosen = jnp.concatenate(
            [rows_of(picks_ref[row]), rows_of(picks_ref[fine_rows + row])], axis=0
        )
        half_done[u * PAIR : (u + 1) * PAIR, :] = jnp.dot(
            left_ref[u * PAIR : (u + 1) * PAIR, :], chosen, preferred_element_type=jnp.float32
        ).astype(jnp.bfloat16)
    for side in range(right.shape[0]):
        span = slice(side * side_width, (side + 1) * side_width)
        out_ref[:, :, span] = jnp.dot(
            half_done[:, span], right[side], preferred_element_type=jnp.float32
        ).reshape(per_step, PAIR, side_width)


def fine_rows_of(picks, gathered, left, piece):
    fine_rows = picks.shape[0] // 2
    n, width = gathered.shape[0], gathered.shape[2]
    per_step = 8
    groups = max(piece, PAIR) // min(piece, PAIR)
    return pl.pallas_call(
        functools.partial(fine_kernel, per_step, fine_rows, piece),
        grid_spec=pltpu.PrefetchScalarGridSpec(
            num_scalar_prefetch=1,
            grid=(fine_rows // per_step,),
            in_specs=[
                pl.BlockSpec(memory_space=pltpu.VMEM),
                pl.BlockSpec((per_step * PAIR, 2 * PAIR), lambda s, picks: (s, 0)),
            ],
            out_specs=pl.BlockSpec((per_step, PAIR, width), lambda s, picks: (s, 0, 0)),
            scratch_shapes=[
                pltpu.VMEM((groups, n * COL_ROWS, width), jnp.bfloat16),
                pltpu.VMEM((2, width // 2, width // 2), jnp.bfloat16),
                pltpu.VMEM((per_step * PAIR, width), jnp.bfloat16),
            ],
        ),
        out_shape=jax.ShapeDtypeStruct((fine_rows, PAIR, width), jnp.float32),
        compiler_params=pltpu.CompilerParams(
            vmem_limit_bytes=16 * 1024 * 1024 + n * 256 * 1024
        ),
        name="fine_rows",
    )(picks, gathered, left)


def ring_place(chip, chips):
    rung, side = lax.div(chip, 2), lax.rem(chip, 2)
    return (1 - side) * rung + side * (chips - 1 - rung)


def chip_at(place, chips):
    place = lax.rem(place + 2 * chips, chips)
    side = lax.div(place, chips // 2)
    return (1 - side) * (2 * place) + side * (2 * (chips - 1 - place) + 1)


def exchange_kernel(
    n, block_ref, cols_ref, gathered_ref, ring_send, ring_recv, twin_send, twin_recv
):
    me = lax.axis_index("wide")
    chips = n // 2
    core = lax.rem(me, 2)
    place = ring_place(lax.div(me, 2), chips)
    twin = me + 1 - 2 * core
    ahead = 2 * chip_at(place + 1, chips) + core
    behind = 2 * chip_at(place - 1, chips) + core
    targets = (ahead, behind)
    rows, width = block_ref.shape
    fine_cols, piece = cols_ref.shape
    parts = ((0, rows // 2), (rows // 2, rows // 2 + fine_cols))
    far = chips // 2

    barrier = pltpu.get_barrier_semaphore()
    for friend in (ahead, behind, twin):
        pl.semaphore_signal(barrier, inc=1, device_id={"wide": friend}, device_id_type=MESH)
    gathered_ref[me, 0:rows, :] = block_ref[...]
    gathered_ref[me, rows:, :] = jnp.concatenate(
        [cols_ref[...], jnp.zeros((fine_cols, width - piece), jnp.bfloat16)], axis=1
    )
    pl.semaphore_wait(barrier, 3)

    def copy_of(part, source, send, recv, target):
        spot = gathered_ref.at[source, pl.ds(*parts[part])]
        return pltpu.make_async_remote_copy(
            src_ref=spot, dst_ref=spot, send_sem=send, recv_sem=recv,
            device_id={"wide": target}, device_id_type=MESH,
        )

    def ring_copy(way, dist, part, source):
        at = (way, dist - 1, part)
        return copy_of(part, source, ring_send.at[at], ring_recv.at[at], targets[way])

    def twin_copy(way, dist, part, source):
        at = (way, dist, part)
        return copy_of(part, source, twin_send.at[at], twin_recv.at[at], twin)

    sent, coming = [], []

    def start(copy):
        copy.start()
        sent.append(copy)

    def goes(way, dist, part):
        return dist < far or (dist == far and part == way)

    for turn in range(2):
        for way in range(2):
            if goes(way, 1, turn ^ way):
                start(ring_copy(way, 1, turn ^ way, me))
    for part in range(2):
        start(twin_copy(0, 0, part, me))
        coming.append(twin_copy(0, 0, part, twin))
    for dist in range(1, far + 1):
        chip_of = [chip_at(place + (dist if way else -dist), chips) for way in range(2)]
        for turn in range(2):
            arrived = []
            for way in range(2):
                part = turn ^ way
                if not goes(way, dist, part):
                    continue
                mine = 2 * chip_of[way] + core
                ring_copy(way, dist, part, mine).wait_recv()
                if goes(way, dist + 1, part):
                    start(ring_copy(way, dist + 1, part, mine))
                arrived.append((way, part, mine))
            for way, part, mine in arrived:
                start(twin_copy(way, dist, part, mine))
                coming.append(twin_copy(way, dist, part, mine + 1 - 2 * core))
    for copy in coming:
        copy.wait_recv()
    for copy in sent:
        copy.wait_send()


def exchange(block, cols, n):
    rows, width = block.shape
    far = n // 4
    total = n * (rows + COL_ROWS) * width * 2
    return pl.pallas_call(
        functools.partial(exchange_kernel, n),
        out_shape=jax.ShapeDtypeStruct((n, rows + COL_ROWS, width), jnp.bfloat16),
        in_specs=[
            pl.BlockSpec(memory_space=pltpu.VMEM),
            pl.BlockSpec(memory_space=pltpu.VMEM),
        ],
        out_specs=pl.BlockSpec(memory_space=pltpu.VMEM),
        scratch_shapes=[
            pltpu.SemaphoreType.DMA((2, far, 2)),
            pltpu.SemaphoreType.DMA((2, far, 2)),
            pltpu.SemaphoreType.DMA((2, far + 1, 2)),
            pltpu.SemaphoreType.DMA((2, far + 1, 2)),
        ],
        compiler_params=pltpu.CompilerParams(
            collective_id=0, has_side_effects=True, vmem_limit_bytes=total + 6 * 1024 * 1024
        ),
        name="exchange",
    )(block, cols)


def per_device(kernel_coarse, row_coeffs, col_coeffs, column_coarse, row_coarse):
    n = lax.axis_size("wide")
    coarse = kernel_coarse.reshape(kernel_coarse.shape[0] * PAIR, -1)
    gathered = exchange(pick(column_coarse, coarse), col_coeffs, n)
    fine_rows = row_coeffs.shape[0]
    left = row_coeffs.reshape(fine_rows, 2, PAIR, PAIR).transpose(0, 3, 1, 2)
    left = left.reshape(fine_rows * PAIR, 2 * PAIR)
    return fine_rows_of(row_coarse.T.reshape(-1), gathered, left, col_coeffs.shape[1])


def solution(mesh):
    in_specs = (
        P(("groups", "wide"), None, None),
        P(("groups", "wide"), None, None),
        P("groups", "wide"),
        P("groups"),
        P(("groups", "wide"), None),
    )
    out_specs = P(("groups", "wide"), None, None)
    return jax.shard_map(
        per_device, mesh=mesh, in_specs=in_specs, out_specs=out_specs, check_vma=False
    )
```

time: 99.6 us -> 34.4 us (0.35)
  waiting for transfers between devices: 36.6 us -> 0 us
  Pallas kernels: 4.81 us -> 29.5 us
  blocking collectives: 23.6 us -> 0 us
  between operations: 13.5 us -> 0.04 us
  local copies, waits for them, and re-layouts: 15.1 us -> 4.61 us
  other arithmetic: 4.51 us -> 0 us
  matrix products: 1.11 us -> 0 us
    all_gather x1 -> x0, waiting for transfers between devices: 36.6 us -> none  [per_device(): expanded = lax.all_gather(expanded, 'wide', axis=0, tiled=True)]
    pallas_call x1 -> x3, Pallas kernels: 4.81 us -> 29.5 us  [the longest x1 21.4 us: exchange(): pl.pallas_call(functools.partial(exchange_kernel, n), out_shape=jax.Shape...]
    all_gather x1 -> x0, blocking collectives: 23.6 us -> none  [per_device(): whole_cols = lax.all_gather(col_coeffs, 'wide', axis=1, tiled=True)]
    mul x1 -> x0, local copies, waits for them, and re-layouts: 10.9 us -> none  [expand_panel(): col_panel = onehot[:, None, :, None] * col_mats[None, :, :, :]]
    mul x1 -> x0, other arithmetic: 3.84 us -> none  [expand_panel(): col_panel = onehot[:, None, :, None] * col_mats[None, :, :, :]]
    dot_general x1 -> x0, matrix products: 1.11 us -> none  [per_device(): jnp.dot(kernel_coarse.reshape(owned, -1), col_panel, preferred_element_ty...]
    unnamed x11 -> x5, local copies, waits for them, and re-layouts: 2.12 us -> 2.16 us
  transfers between devices with their start and end apart: 1 -> 0, of which waited for: 1 -> 0; matrix products, arithmetic and copies ran while one was open for 2% -> 0% of each run, Pallas kernels for 0% -> 0%
where the time goes in v3:
time: 34.4 us; the launch traced here: 34.2 us
  Pallas kernels  29.5 us (86%)
  local copies, waits for them, and re-layouts  4.61 us (13%)
    pallas_call x1, Pallas kernels, exchange(): pl.pallas_call(functools.partial(exchange_kernel, n), out_shape=jax.Shape...  21.4 us
    pallas_call x1, Pallas kernels, fine_rows_of(): pl.pallas_call(functools.partial(fine_kernel, per_step, fine_rows, piece)...  6.08 us
    unnamed x5, local copies, waits for them, and re-layouts  2.16 us
    pallas_call x1, Pallas kernels, pick(): pl.pallas_call(pick_kernel, out_shape=jax.ShapeDtypeStruct((coarse.shape[...  2.01 us
    reshape x2, local copies, waits for them, and re-layouts, per_device(): left = left.reshape(fine_rows * PAIR, 2 * PAIR)  1.68 us
    reshape x1, local copies, waits for them, and re-layouts, per_device(): row_coarse.T.reshape(-1)  0.77 us

profile of v3, /device:TPU:0, one launch (start us, length us, event | category | flops | bytes accessed | tf_op | source)
XLA Modules:
  0.0 34.2 jit_solution(11409886562196976264)
XLA Ops:
  0.0 0.0 copy-start.1
  0.0 0.8 %reshape.12.picks_ref = s32[128]{0:T(128)S(1)} reshape(s32[2,64]{1,0:T(2,128)} %bitcast.7) | data formatting | bytes 1024 | tf_op jit(solution)/shard_map/reshape | solution.py:271
  0.8 2.0 %pick.1.block_ref = bf16[128,512]{1,0:T(8,128)(2,1)} custom-call(s32[16]{0:T(128)} %column_ref.1, bf16[128,2048]{1,0:T(8,128)(2,1)} %bitcast.6), custom_call_target="tpu_custom_call" | custom-call | tf_op jit(solution)/shard_map/pick/pallas_call | solution.py:41
  2.8 1.3 %copy.7 = bf16[64,2,1024]{0,2,1:T(8,128)(2,1)S(1)} copy(bf16[64,2,1024]{2,1,0:T(2,128)(2,1)} %param.6) | data formatting | bytes 524288 | tf_op args[1]
  4.0 1.2 %copy.10 = bf16[64,32,2,32]{3,2,1,0:T(2,128)(2,1)S(1)} copy(bf16[64,32,2,32]{0,1,3,2:T(8,128)(2,1)S(1)} %bitcast.5) | data formatting | bytes 524288 | tf_op jit(solution)/shard_map/reshape | solution.py:270
  5.2 0.5 %reshape.16.left_ref = bf16[2048,64]{1,0:T(8,128)(2,1)S(1)} reshape(bf16[64,32,2,32]{3,2,1,0:T(2,128)(2,1)S(1)} %copy.10) | data formatting | bytes 524288 | tf_op jit(solution)/shard_map/reshape | solution.py:270
  5.7 0.0 copy-done.1
  5.8 0.0 copy-start
  5.8 0.9 %copy-done = bf16[128,512]{1,0:T(8,128)(2,1)S(1)} copy-done((bf16[128,512]{1,0:T(8,128)(2,1)S(1)}, bf16[128,512]{1,0:T(8,128)(2,1)}, u32[]{:S(2)}) %copy-start) | copy-done | bytes 131096
  6.7 21.4 %exchange.1.gathered_ref = bf16[16,144,512]{2,1,0:T(8,128)(2,1)S(1)} custom-call(bf16[128,512]{1,0:T(8,128)(2,1)S(1)} %copy-done, bf16[16,64]{1,0:T(8,128)(2,1)S(1)} %copy-done.1), custom_call_target="tpu_custom_call" | custom-call | tf_op jit(solution)/shard_map/exchange/pallas_call | solution.py:243
  28.1 6.1 %fine_rows.1 = f32[64,32,512]{2,1,0:T(8,128)} custom-call(s32[128]{0:T(128)S(1)} %reshape.12.picks_ref, bf16[16,144,512]{2,1,0:T(8,128)(2,1)S(1)} %exchange.1.gathered_ref, bf16[2048,64]{1,0:T(8,128)(2,1)S(1)} %reshape.16.left_ref), custom_call_target="tpu_custom_call" | custom-call | tf_op jit(solution)/shard_map/fine_rows/pallas_call | solution.py:126
Async XLA Ops:
  0.0 5.7 %copy-start.1 = (bf16[16,64]{1,0:T(8,128)(2,1)S(1)}, bf16[16,64]{1,0:T(8,128)(2,1)}, u32[]{:S(2)}) copy-start(bf16[16,64]{1,0:T(8,128)(2,1)} %cols_ref.1) | copy-start | bytes 6148
  5.8 0.9 %copy-start = (bf16[128,512]{1,0:T(8,128)(2,1)S(1)}, bf16[128,512]{1,0:T(8,128)(2,1)}, u32[]{:S(2)}) copy-start(bf16[128,512]{1,0:T(8,128)(2,1)} %pick.1.block_ref) | copy-start | bytes 393220

commit v4 on v3

--- a/solution.py
+++ b/solution.py
@@ -8,6 +8,8 @@
 from jax.sharding import PartitionSpec as P
 
 PAIR = 32
+SLOTS = 4
+TEAM = 4
 COL_ROWS = 16
 MESH = pl.DeviceIdType.MESH
 
@@ -20,7 +22,7 @@
     return jnp.where(mask, 1.0, 0.0).astype(jnp.bfloat16)
 
 
-def pick_kernel(column_ref, coarse_ref, picked_ref):
+def pick_kernel(column_ref, coarse_ref, after_ref, picked_ref):
     lane_gap = iota((128, 128), 0) - iota((128, 128), 1)
     lane_group = lax.div(iota((128, 128), 1), PAIR)
     for block in range(picked_ref.shape[1] // 128):
@@ -37,16 +39,21 @@
             preferred_element_type=jnp.float32,
         ).astype(jnp.bfloat16)
 
-def pick(column_coarse, coarse):
+def pick(column_coarse, coarse, after):
     return pl.pallas_call(
         pick_kernel,
         out_shape=jax.ShapeDtypeStruct(
             (coarse.shape[0], column_coarse.shape[0] * PAIR), jnp.bfloat16
         ),
-        in_specs=[pl.BlockSpec(memory_space=pltpu.SMEM), pl.BlockSpec(memory_space=pltpu.VMEM)],
+        in_specs=[
+            pl.BlockSpec(memory_space=pltpu.SMEM),
+            pl.BlockSpec(memory_space=pltpu.VMEM),
+            pl.BlockSpec(memory_space=pl.ANY),
+        ],
         out_specs=pl.BlockSpec(memory_space=pltpu.VMEM),
+        compiler_params=pltpu.CompilerParams(vmem_limit_bytes=4 * 1024 * 1024),
         name="pick",
-    )(column_coarse, coarse)
+    )(column_coarse, coarse, after)
 
 
 def spread_cols(piece, gathered_ref, spread, right):
@@ -88,57 +95,81 @@
 
 
 def fine_kernel(
-    per_step, fine_rows, piece, picks_ref, gathered_ref, left_ref, out_ref, spread, right, half_done
+    per_step, piece, picks_ref, gathered_ref, left_ref, out_ref, spread, right, half_done, done, sent
 ):
-    step = pl.program_id(0)
     owned = (gathered_ref.shape[1] - COL_ROWS) // PAIR
     side_width = right.shape[1]
 
-    @pl.when(step == 0)
-    def _():
-        spread_cols(piece, gathered_ref, spread, right)
+    spread_cols(piece, gathered_ref, spread, right)
 
     def rows_of(coarse):
         owner = lax.div(coarse, owned)
         first = pl.multiple_of((coarse - owner * owned) * PAIR, PAIR)
         return gathered_ref[owner, pl.ds(first, PAIR), :]
 
-    for u in range(per_step):
-        row = step * per_step + u
-        chosen = jnp.concatenate(
-            [rows_of(picks_ref[row]), rows_of(picks_ref[fine_rows + row])], axis=0
-        )
-        half_done[u * PAIR : (u + 1) * PAIR, :] = jnp.dot(
-            left_ref[u * PAIR : (u + 1) * PAIR, :], chosen, preferred_element_type=jnp.float32
-        ).astype(jnp.bfloat16)
-    for side in range(right.shape[0]):
-        span = slice(side * side_width, (side + 1) * side_width)
-        out_ref[:, :, span] = jnp.dot(
-            half_done[:, span], right[side], preferred_element_type=jnp.float32
-        ).reshape(per_step, PAIR, side_width)
+    shape = (TEAM * PAIR, TEAM * 2 * PAIR)
+    same_row = lax.div(iota(shape, 0), PAIR) == lax.div(iota(shape, 1), 2 * PAIR)
+    steps = out_ref.shape[0] // per_step
+
+    def send(step):
+        at = pl.ds(step * per_step, per_step)
+        return pltpu.make_async_copy(done.at[step % SLOTS], out_ref.at[at], sent.at[step % SLOTS])
+
+    def one_step(step, carry):
+        if step >= SLOTS:
+            send(step - SLOTS).wait()
+
+        for team in range(per_step // TEAM):
+            chosen = []
+            for u in range(TEAM):
+                row = step * per_step + team * TEAM + u
+                chosen += [rows_of(picks_ref[0, row]), rows_of(picks_ref[1, row])]
+            first = (step * per_step + team * TEAM) * PAIR
+            left = jnp.concatenate([left_ref[pl.ds(first, TEAM * PAIR), :]] * TEAM, axis=1)
+            half_done[step % 2, team * TEAM * PAIR : (team + 1) * TEAM * PAIR, :] = jnp.dot(
+                jnp.where(same_row, left, jnp.zeros_like(left)),
+                jnp.concatenate(chosen, axis=0),
+                preferred_element_type=jnp.float32,
+            ).astype(jnp.bfloat16)
+        for side in range(right.shape[0]):
+            span = slice(side * side_width, (side + 1) * side_width)
+            done[step % SLOTS, :, :, span] = jnp.dot(
+                half_done[step % 2, :, span], right[side], preferred_element_type=jnp.float32
+            ).reshape(per_step, PAIR, side_width)
+        send(step).start()
+        return carry
+
+    for step in range(steps):
+        one_step(step, 0)
+
+    def finish(step, carry):
+        send(step).wait()
+        return carry
+
+    for step in range(steps - SLOTS, steps):
+        finish(step, 0)
 
 
 def fine_rows_of(picks, gathered, left, piece):
-    fine_rows = picks.shape[0] // 2
+    fine_rows = picks.shape[1]
     n, width = gathered.shape[0], gathered.shape[2]
-    per_step = 8
+    per_step = 16
     groups = max(piece, PAIR) // min(piece, PAIR)
     return pl.pallas_call(
-        functools.partial(fine_kernel, per_step, fine_rows, piece),
-        grid_spec=pltpu.PrefetchScalarGridSpec(
-            num_scalar_prefetch=1,
-            grid=(fine_rows // per_step,),
-            in_specs=[
-                pl.BlockSpec(memory_space=pltpu.VMEM),
-                pl.BlockSpec((per_step * PAIR, 2 * PAIR), lambda s, picks: (s, 0)),
-            ],
-            out_specs=pl.BlockSpec((per_step, PAIR, width), lambda s, picks: (s, 0, 0)),
-            scratch_shapes=[
-                pltpu.VMEM((groups, n * COL_ROWS, width), jnp.bfloat16),
-                pltpu.VMEM((2, width // 2, width // 2), jnp.bfloat16),
-                pltpu.VMEM((per_step * PAIR, width), jnp.bfloat16),
-            ],
-        ),
+        functools.partial(fine_kernel, per_step, piece),
+        in_specs=[
+            pl.BlockSpec(memory_space=pltpu.SMEM),
+            pl.BlockSpec(memory_space=pltpu.VMEM),
+            pl.BlockSpec(memory_space=pltpu.VMEM),
+        ],
+        out_specs=pl.BlockSpec(memory_space=pl.ANY),
+        scratch_shapes=[
+            pltpu.VMEM((groups, n * COL_ROWS, width), jnp.bfloat16),
+            pltpu.VMEM((2, width // 2, width // 2), jnp.bfloat16),
+            pltpu.VMEM((2, per_step * PAIR, width), jnp.bfloat16),
+            pltpu.VMEM((SLOTS, per_step, PAIR, width), jnp.float32),
+            pltpu.SemaphoreType.DMA((SLOTS,)),
+        ],
         out_shape=jax.ShapeDtypeStruct((fine_rows, PAIR, width), jnp.float32),
         compiler_params=pltpu.CompilerParams(
             vmem_limit_bytes=16 * 1024 * 1024 + n * 256 * 1024
@@ -264,11 +295,11 @@
 def per_device(kernel_coarse, row_coeffs, col_coeffs, column_coarse, row_coarse):
     n = lax.axis_size("wide")
     coarse = kernel_coarse.reshape(kernel_coarse.shape[0] * PAIR, -1)
-    gathered = exchange(pick(column_coarse, coarse), col_coeffs, n)
     fine_rows = row_coeffs.shape[0]
     left = row_coeffs.reshape(fine_rows, 2, PAIR, PAIR).transpose(0, 3, 1, 2)
     left = left.reshape(fine_rows * PAIR, 2 * PAIR)
-    return fine_rows_of(row_coarse.T.reshape(-1), gathered, left, col_coeffs.shape[1])
+    gathered = exchange(pick(column_coarse, coarse, left), col_coeffs, n)
+    return fine_rows_of(row_coarse.T, gathered, left, col_coeffs.shape[1])
 
 
 def solution(mesh):

time: 34.4 us -> 29.8 us (0.87)
  Pallas kernels: 29.5 us -> 25.9 us
  local copies, waits for them, and re-layouts: 4.61 us -> 3.66 us
    pallas_call x1, Pallas kernels: 6.08 us -> 3.49 us  [fine_rows_of(): pl.pallas_call(functools.partial(fine_kernel, per_step, piece), in_specs=...]
    pallas_call x1, Pallas kernels: 2.01 us -> 0.85 us  [pick(): pl.pallas_call(pick_kernel, out_shape=jax.ShapeDtypeStruct((coarse.shape[...]
    reshape x1 -> x0, local copies, waits for them, and re-layouts: 0.77 us -> none  [per_device(): row_coarse.T.reshape(-1)]
    unnamed x5 -> x9, local copies, waits for them, and re-layouts: 2.16 us -> 1.98 us
where the time goes in v4:
time: 29.8 us; the launch traced here: 29.6 us
  Pallas kernels  25.9 us (87%)
  local copies, waits for them, and re-layouts  3.66 us (12%)
    pallas_call x1, Pallas kernels, exchange(): pl.pallas_call(functools.partial(exchange_kernel, n), out_shape=jax.Shape...  21.6 us
    pallas_call x1, Pallas kernels, fine_rows_of(): pl.pallas_call(functools.partial(fine_kernel, per_step, piece), in_specs=...  3.49 us
    unnamed x9, local copies, waits for them, and re-layouts  1.98 us
    reshape x2, local copies, waits for them, and re-layouts, per_device(): left = left.reshape(fine_rows * PAIR, 2 * PAIR)  1.68 us
    pallas_call x1, Pallas kernels, pick(): pl.pallas_call(pick_kernel, out_shape=jax.ShapeDtypeStruct((coarse.shape[...  0.85 us

profile of v4, /device:TPU:0, one launch (start us, length us, event | category | flops | bytes accessed | tf_op | source)
XLA Modules:
  0.0 29.6 jit_solution(11366576406460858780)
XLA Ops:
  0.0 0.0 copy-start.2
  0.0 0.0 copy-start.1
  0.0 0.0 copy-start
  0.0 1.3 %copy.7 = bf16[64,2,1024]{0,2,1:T(8,128)(2,1)S(1)} copy(bf16[64,2,1024]{2,1,0:T(2,128)(2,1)} %param.6) | data formatting | bytes 524288 | tf_op args[1]
  1.3 1.2 %copy.11 = bf16[64,32,2,32]{3,2,1,0:T(2,128)(2,1)S(1)} copy(bf16[64,32,2,32]{0,1,3,2:T(8,128)(2,1)S(1)} %bitcast.7) | data formatting | bytes 524288 | tf_op jit(solution)/shard_map/reshape | solution.py:300
  2.5 0.5 %reshape.12.after_ref.left_ref = bf16[2048,64]{1,0:T(8,128)(2,1)S(1)} reshape(bf16[64,32,2,32]{3,2,1,0:T(2,128)(2,1)S(1)} %copy.11) | data formatting | bytes 524288 | tf_op jit(solution)/shard_map/reshape | solution.py:300
  3.0 0.0 copy-done
  3.0 0.0 copy-start.3
  3.0 0.6 %copy-done.3 = s32[16]{0:T(128)S(1)} copy-done((s32[16]{0:T(128)S(1)}, s32[16]{0:T(128)}, u32[]{:S(2)}) %copy-start.3) | copy-done | bytes 88
  3.7 0.8 %pick.1.block_ref = bf16[128,512]{1,0:T(8,128)(2,1)S(1)} custom-call(s32[16]{0:T(128)S(1)} %copy-done.3, bf16[128,2048]{1,0:T(8,128)(2,1)S(1)} %bitcast.5, bf16[2048,64]{1,0:T(8,128)(2,1)S(1)} %reshape.12.after_ref.left_ref), custom_call_target="tpu_custom_call" | custom-call | tf_op jit(solution)/shard_map/pick/pallas_call | solution.py:43
  4.5 0.0 copy-done.1
  4.6 21.6 %exchange.1.gathered_ref = bf16[16,144,512]{2,1,0:T(8,128)(2,1)S(1)} custom-call(bf16[128,512]{1,0:T(8,128)(2,1)S(1)} %pick.1.block_ref, bf16[16,64]{1,0:T(8,128)(2,1)S(1)} %copy-done.1), custom_call_target="tpu_custom_call" | custom-call | tf_op jit(solution)/shard_map/exchange/pallas_call | solution.py:274
  26.1 0.0 copy-done.2
  26.2 3.5 %fine_rows.1 = f32[64,32,512]{2,1,0:T(8,128)} custom-call(s32[2,64]{1,0:T(2,128)S(1)} %bitcast.6, bf16[16,144,512]{2,1,0:T(8,128)(2,1)S(1)} %exchange.1.gathered_ref, bf16[2048,64]{1,0:T(8,128)(2,1)S(1)} %reshape.12.after_ref.left_ref), custom_call_target="tpu_custom_call" | custom-call | tf_op jit(solution)/shard_map/fine_rows/pallas_call | solution.py:158
Async XLA Ops:
  0.0 26.1 %copy-start.2 = (s32[64,2]{0,1:T(2,128)S(1)}, s32[64,2]{0,1:T(2,128)}, u32[]{:S(2)}) copy-start(s32[64,2]{0,1:T(2,128)} %param.9) | copy-start | bytes 1540
  0.0 4.5 %copy-start.1 = (bf16[16,64]{1,0:T(8,128)(2,1)S(1)}, bf16[16,64]{1,0:T(8,128)(2,1)}, u32[]{:S(2)}) copy-start(bf16[16,64]{1,0:T(8,128)(2,1)} %cols_ref.1) | copy-start | bytes 6148
  0.0 3.0 %copy-start = (bf16[4,32,2048]{2,1,0:T(8,128)(2,1)S(1)}, bf16[4,32,2048]{2,1,0:T(8,128)(2,1)}, u32[]{:S(2)}) copy-start(bf16[4,32,2048]{2,1,0:T(8,128)(2,1)} %param.5) | copy-start | bytes 1572868
  3.0 0.7 %copy-start.3 = (s32[16]{0:T(128)S(1)}, s32[16]{0:T(128)}, u32[]{:S(2)}) copy-start(s32[16]{0:T(128)} %column_ref.1) | copy-start | bytes 196

commit v5 on v4

--- a/solution.py
+++ b/solution.py
@@ -95,12 +95,16 @@
 
 
 def fine_kernel(
-    per_step, piece, picks_ref, gathered_ref, left_ref, out_ref, spread, right, half_done, done, sent
+    per_step, piece, picks_hbm, gathered_ref, left_ref, out_ref,
+    spread, right, half_done, done, sent, picks_ref, fetched,
 ):
     owned = (gathered_ref.shape[1] - COL_ROWS) // PAIR
     side_width = right.shape[1]
 
+    fetch = pltpu.make_async_copy(picks_hbm, picks_ref, fetched)
+    fetch.start()
     spread_cols(piece, gathered_ref, spread, right)
+    fetch.wait()
 
     def rows_of(coarse):
         owner = lax.div(coarse, owned)
@@ -158,7 +162,7 @@
     return pl.pallas_call(
         functools.partial(fine_kernel, per_step, piece),
         in_specs=[
-            pl.BlockSpec(memory_space=pltpu.SMEM),
+            pl.BlockSpec(memory_space=pl.ANY),
             pl.BlockSpec(memory_space=pltpu.VMEM),
             pl.BlockSpec(memory_space=pltpu.VMEM),
         ],
@@ -169,6 +173,8 @@
             pltpu.VMEM((2, per_step * PAIR, width), jnp.bfloat16),
             pltpu.VMEM((SLOTS, per_step, PAIR, width), jnp.float32),
             pltpu.SemaphoreType.DMA((SLOTS,)),
+            pltpu.SMEM(picks.shape, jnp.int32),
+            pltpu.SemaphoreType.DMA,
         ],
         out_shape=jax.ShapeDtypeStruct((fine_rows, PAIR, width), jnp.float32),
         compiler_params=pltpu.CompilerParams(

time: 29.8 us -> 29.5 us (0.990)
  Pallas kernels: 25.9 us -> 25.6 us
    pallas_call x1, Pallas kernels: 3.49 us -> 3.18 us  [fine_rows_of(): pl.pallas_call(functools.partial(fine_kernel, per_step, piece), in_specs=...]
where the time goes in v5:
time: 29.5 us; the launch traced here: 29.3 us
  Pallas kernels  25.6 us (87%)
  local copies, waits for them, and re-layouts  3.66 us (12%)
    pallas_call x1, Pallas kernels, exchange(): pl.pallas_call(functools.partial(exchange_kernel, n), out_shape=jax.Shape...  21.6 us
    pallas_call x1, Pallas kernels, fine_rows_of(): pl.pallas_call(functools.partial(fine_kernel, per_step, piece), in_specs=...  3.18 us
    unnamed x9, local copies, waits for them, and re-layouts  1.98 us
    reshape x2, local copies, waits for them, and re-layouts, per_device(): left = left.reshape(fine_rows * PAIR, 2 * PAIR)  1.68 us
    pallas_call x1, Pallas kernels, pick(): pl.pallas_call(pick_kernel, out_shape=jax.ShapeDtypeStruct((coarse.shape[...  0.85 us

profile of v5, /device:TPU:0, one launch (start us, length us, event | category | flops | bytes accessed | tf_op | source)
XLA Modules:
  0.0 29.3 jit_solution(6073312775169268648)
XLA Ops:
  0.0 0.0 copy-start.2
  0.0 0.0 copy-start.1
  0.0 0.0 copy-start
  0.0 1.3 %copy.7 = bf16[64,2,1024]{0,2,1:T(8,128)(2,1)S(1)} copy(bf16[64,2,1024]{2,1,0:T(2,128)(2,1)} %param.6) | data formatting | bytes 524288 | tf_op args[1]
  1.3 1.2 %copy.11 = bf16[64,32,2,32]{3,2,1,0:T(2,128)(2,1)S(1)} copy(bf16[64,32,2,32]{0,1,3,2:T(8,128)(2,1)S(1)} %bitcast.7) | data formatting | bytes 524288 | tf_op jit(solution)/shard_map/reshape | solution.py:306
  2.5 0.5 %reshape.12.after_ref.left_ref = bf16[2048,64]{1,0:T(8,128)(2,1)S(1)} reshape(bf16[64,32,2,32]{3,2,1,0:T(2,128)(2,1)S(1)} %copy.11) | data formatting | bytes 524288 | tf_op jit(solution)/shard_map/reshape | solution.py:306
  3.0 0.0 copy-done
  3.0 0.0 copy-start.3
  3.0 0.6 %copy-done.3 = s32[16]{0:T(128)S(1)} copy-done((s32[16]{0:T(128)S(1)}, s32[16]{0:T(128)}, u32[]{:S(2)}) %copy-start.3) | copy-done | bytes 88
  3.7 0.8 %pick.1.block_ref = bf16[128,512]{1,0:T(8,128)(2,1)S(1)} custom-call(s32[16]{0:T(128)S(1)} %copy-done.3, bf16[128,2048]{1,0:T(8,128)(2,1)S(1)} %bitcast.5, bf16[2048,64]{1,0:T(8,128)(2,1)S(1)} %reshape.12.after_ref.left_ref), custom_call_target="tpu_custom_call" | custom-call | tf_op jit(solution)/shard_map/pick/pallas_call | solution.py:43
  4.5 0.0 copy-done.1
  4.6 21.6 %exchange.1.gathered_ref = bf16[16,144,512]{2,1,0:T(8,128)(2,1)S(1)} custom-call(bf16[128,512]{1,0:T(8,128)(2,1)S(1)} %pick.1.block_ref, bf16[16,64]{1,0:T(8,128)(2,1)S(1)} %copy-done.1), custom_call_target="tpu_custom_call" | custom-call | tf_op jit(solution)/shard_map/exchange/pallas_call | solution.py:280
  26.1 0.0 copy-done.2
  26.2 3.2 %fine_rows.1 = f32[64,32,512]{2,1,0:T(8,128)} custom-call(s32[2,64]{1,0:T(2,128)S(1)} %bitcast.6, bf16[16,144,512]{2,1,0:T(8,128)(2,1)S(1)} %exchange.1.gathered_ref, bf16[2048,64]{1,0:T(8,128)(2,1)S(1)} %reshape.12.after_ref.left_ref), custom_call_target="tpu_custom_call" | custom-call | tf_op jit(solution)/shard_map/fine_rows/pallas_call | solution.py:162
Async XLA Ops:
  0.0 26.1 %copy-start.2 = (s32[64,2]{0,1:T(2,128)S(1)}, s32[64,2]{0,1:T(2,128)}, u32[]{:S(2)}) copy-start(s32[64,2]{0,1:T(2,128)} %param.9) | copy-start | bytes 1540
  0.0 4.5 %copy-start.1 = (bf16[16,64]{1,0:T(8,128)(2,1)S(1)}, bf16[16,64]{1,0:T(8,128)(2,1)}, u32[]{:S(2)}) copy-start(bf16[16,64]{1,0:T(8,128)(2,1)} %cols_ref.1) | copy-start | bytes 6148
  0.0 3.0 %copy-start = (bf16[4,32,2048]{2,1,0:T(8,128)(2,1)S(1)}, bf16[4,32,2048]{2,1,0:T(8,128)(2,1)}, u32[]{:S(2)}) copy-start(bf16[4,32,2048]{2,1,0:T(8,128)(2,1)} %param.5) | copy-start | bytes 1572868
  3.0 0.7 %copy-start.3 = (s32[16]{0:T(128)S(1)}, s32[16]{0:T(128)}, u32[]{:S(2)}) copy-start(s32[16]{0:T(128)} %column_ref.1) | copy-start | bytes 196
